TPU v7x, 512 devices: a whole 4x8x8 slice. The times are simulated.
512 devices in a mesh: sub: 16 (over x_lo, z), inner: 32 (over x_hi, y, core).
Axes of the slice: x: 4 (x_hi: 2, x_lo: 2; x = x_hi * 2 + x_lo), y: 8, z: 8, core: 2. Of those that a mesh axis runs over, the one named last changes fastest.
Arguments:
- front_leaf: bfloat16 [327680, 1024], P(('sub', 'inner')), may hold values from -6 to 6
- front_mid: bfloat16 [327680, 1024], P(('sub', 'inner')), may hold values from -6 to 6
- front_top: bfloat16 [327680, 1024], P(('sub', 'inner')), may hold values from -6 to 6
- dinv_leaf: bfloat16 [8192, 256], P('sub'), may hold values from -0.046875 to 0.046875
- dinv_mid: bfloat16 [4096, 256], P('sub'), may hold values from -0.046875 to 0.046875
- dinv_top: bfloat16 [2048, 256], P('sub'), may hold values from -0.046875 to 0.046875
- live_rows: int32 [3, 512], P(None, ('sub', 'inner')), may hold values from 320 to 640, as said below
- map_leaf: int32 [327680], P(('sub', 'inner')), may hold values from 0 to 1279, as said below
- map_mid: int32 [327680], P(('sub', 'inner')), may hold values from 0 to 1279, as said below
Outputs:
- contribution: bfloat16 [327680, 512], P(('sub', 'inner'))
Inputs may be any that keep to these rules, and one draw needn't show every extreme that they name: `live_rows`: at each level some device block has all 640 rows live. `map_leaf`: within each block of 640 consecutive entries the codes are distinct and exactly half of them are 640 or more. `map_mid`: within each block of 640 consecutive entries the codes are distinct and exactly half of them are 640 or more.
All inputs are finite; a program needn't handle non-finite values.
Results may differ from a plain program's by a relative error of at most 0.0065.
Values may be sent and summed in bfloat16 or wider, within the bound.
A program may use at most 64 MiB of HBM per device.

v0:
```python
import jax
import jax.numpy as jnp
from jax import lax
from jax.sharding import PartitionSpec as P

PANEL = 512
BLOCK = 256
NEXT = 512


def swapped(value, axis, bit):
    return lax.ppermute(value, axis, [(i, i ^ 1 << bit) for i in range(lax.axis_size(axis))])


def sent_to_all(value, axis):
    count = lax.axis_size(axis)
    return lax.all_to_all(
        jnp.broadcast_to(value[None], (count, *value.shape)), axis, 0, 0, tiled=True
    )


def in_order(tiles, dim):
    tiles = jnp.moveaxis(tiles, 0, dim)
    lengths = tiles.shape
    return tiles.reshape(*lengths[:dim], lengths[dim] * lengths[dim + 1], *lengths[dim + 2 :])


def gathered_copies(value, axis, dim):
    tiles = sent_to_all(value, axis)
    return in_order(tiles, dim)


def join_halves(mine_part, other_part, bit_index):
    lower_side = lax.axis_index("sub") >> bit_index & 1 == 0
    return jnp.where(
        lower_side,
        jnp.concatenate([mine_part, other_part], 0),
        jnp.concatenate([other_part, mine_part], 0),
    )


def full_inverse(inv_shard, levels):
    whole_part = inv_shard
    for bit_index in range(levels):
        other_part = swapped(whole_part, "sub", bit_index)
        whole_part = join_halves(whole_part, other_part, bit_index)
    return whole_part


def swap_pivots(pivots, bit_index):
    other_part = swapped(pivots, "sub", bit_index)
    return join_halves(pivots, other_part, bit_index)


def factor_level(front_block, inverse, live_count, level_index):
    row_count = front_block.shape[0]
    block_count = PANEL // BLOCK
    panel_part = front_block[:, :PANEL].reshape(row_count, block_count, BLOCK)
    inv_table = inverse.reshape(block_count, BLOCK, BLOCK)
    live_mask = lax.broadcasted_iota(jnp.int32, (row_count, 1), 0) < live_count
    factor = jnp.einsum(
        "rbk,bjk->rbj", panel_part, inv_table, preferred_element_type=jnp.float32
    ).reshape(row_count, PANEL)
    factor = jnp.where(live_mask, factor, 0.0).astype(jnp.bfloat16)
    inner_count = lax.axis_size("inner")
    pivot_count = NEXT // (inner_count << level_index)
    local_pivots = factor[:pivot_count]
    pivots = gathered_copies(local_pivots, "inner", 0)
    for bit_index in range(level_index):
        pivots = swap_pivots(pivots, bit_index)
    product = lax.dot_general(
        factor, pivots, (((1,), (1,)), ((), ())), preferred_element_type=jnp.float32
    )
    update = jnp.where(live_mask, front_block[:, PANEL:].astype(jnp.float32) - product, 0.0)
    return update.astype(jnp.bfloat16)


def extend_add(update, code_map, parent, level_index):
    row_count = update.shape[0]
    col_count = update.shape[1]
    half_rows = row_count // 2
    outward = code_map >= row_count
    own_index = jnp.where(outward, row_count, code_map)
    own_sum = (
        jnp.zeros((row_count, col_count), jnp.float32)
        .at[own_index]
        .add(update.astype(jnp.float32), mode="drop")
    )
    position = jnp.cumsum(outward.astype(jnp.int32)) - 1
    target_slot = jnp.where(outward, position, half_rows)
    picked = (
        jnp.zeros((half_rows,), jnp.int32)
        .at[target_slot]
        .set(lax.iota(jnp.int32, row_count), mode="drop")
    )
    sent_rows = update[picked]
    sent_target = code_map[picked] - row_count
    got_rows, got_target = swapped((sent_rows, sent_target), "sub", level_index)
    far_sum = (
        jnp.zeros((row_count, col_count), jnp.float32)
        .at[got_target]
        .add(got_rows.astype(jnp.float32))
    )
    merged = parent[:, :col_count].astype(jnp.float32) + own_sum + far_sum
    return jnp.concatenate([merged.astype(jnp.bfloat16), parent[:, col_count:]], 1)


def per_device(
    front_leaf, front_mid, front_top, dinv_leaf, dinv_mid, dinv_top, live_rows, map_leaf, map_mid
):
    inverse_mid = full_inverse(dinv_mid, 1)
    inverse_top = full_inverse(dinv_top, 2)
    update = factor_level(front_leaf, dinv_leaf, live_rows[0, 0], 0)
    parent = extend_add(update, map_leaf, front_mid, 0)
    update = factor_level(parent, inverse_mid, live_rows[1, 0], 1)
    parent = extend_add(update, map_mid, front_top, 1)
    return factor_level(parent, inverse_top, live_rows[2, 0], 2)


def solution(mesh):
    placed = (
        P(("sub", "inner"), None),
        P(("sub", "inner"), None),
        P(("sub", "inner"), None),
        P("sub", None),
        P("sub", None),
        P("sub", None),
        P(None, ("sub", "inner")),
        P(("sub", "inner")),
        P(("sub", "inner")),
    )
    return jax.shard_map(
        per_device, mesh=mesh, in_specs=placed, out_specs=P(("sub", "inner"), None), check_vma=False
    )
```

profile of v0, /device:TPU:1, one launch (start us, length us, event | category | flops | bytes accessed | tf_op | source)
XLA Modules:
  0.0 161.1 jit_solution(4497740571169923108)
XLA Ops:
  4.9 11.2 %all-to-all-start = ((bf16[32,16,512]{2,1,0:T(8,128)(2,1)}), bf16[32,16,512]{2,1,0:T(8,128)(2,1)S(1)}, u32[]{:S(2)}, u32[]{:S(2)}) async-start(bf16[32,16,512]{2,1,0:T(8,128)(2,1)} %broadcast_in_dim.94), calls=%async_computation | async-start | bytes 1048576 | tf_op jit(solution)/shard_map/all_to_all | solution.py:17
  17.2 4.1 %scatter_custom_fusion.1 = s32[320]{0:T(512)S(1)} fusion(s32[640]{0:T(1024)S(1)} %get-tuple-element.7, s32[640]{0:T(1024)S(1)} %iota.25, s32[]{:T(128)} %constant.12.clone.1), kind=kCustom, calls=%fused_computation.87 | custom fusion | bytes 1284 | tf_op jit(solution)/shard_map/scatter | solution.py:94
  23.6 4.0 %collective-permute-start.3 = (s32[320]{0:T(512)}, s32[320]{0:T(512)}, u32[]{:S(2)}, u32[]{:S(2)}) collective-permute-start(s32[320]{0:T(512)} %broadcast_add_fusion.1), channel_id=1, source_target_pairs={{0,32},{32,0},{64,96},{96,64},{128,160},{160,128},{192,224},{224,1... | collective-permute-start | bytes 3848 | tf_op jit(solution)/shard_map/ppermute | solution.py:12
  27.6 1.9 %collective-permute-start.2 = (bf16[256,256]{1,0:T(8,128)(2,1)}, bf16[256,256]{1,0:T(8,128)(2,1)}, u32[]{:S(2)}, u32[]{:S(2)}) collective-permute-start(bf16[256,256]{1,0:T(8,128)(2,1)} %param.13), channel_id=1, source_target_pairs={{0,32},{32,0},{64,96},{96,64},{128,160},{160,128},{192,224},{224,1... | collective-permute-start | bytes 393224 | tf_op jit(solution)/shard_map/ppermute | solution.py:12
  30.2 4.1 %scatter_custom_fusion.4 = s32[320]{0:T(512)S(1)} fusion(s32[640]{0:T(1024)S(1)} %get-tuple-element.5, s32[640]{0:T(1024)S(1)} %iota.26, s32[]{:T(128)} %constant.12.clone.1), kind=kCustom, calls=%fused_computation.85 | custom fusion | bytes 1284 | tf_op jit(solution)/shard_map/scatter | solution.py:94
  39.4 2.0 %gather_fusion.1 = bf16[320,512]{1,0:T(8,128)(2,1)S(1)} fusion(bf16[640,512]{1,0:T(8,128)(2,1)S(1)} %fusion.3, s32[1024]{0:T(1024)S(1)} %pad_clamp_fusion.1), kind=kCustom, calls=%fused_computation.1 | custom fusion | bytes 656640 | tf_op jit(solution)/shard_map/gather | solution.py:96
  41.4 3.4 %collective-permute-start.4 = (bf16[320,512]{1,0:T(8,128)(2,1)S(1)}, bf16[320,512]{1,0:T(8,128)(2,1)S(1)}, u32[]{:S(2)}, u32[]{:S(2)}) collective-permute-start(bf16[320,512]{1,0:T(8,128)(2,1)S(1)} %gather_fusion.1), channel_id=1, source_target_pairs={{0,32},{32,0},{64,96},{96,64},{128,160},{160,128},{192,224},{224,1... | collective-permute-start | bytes 983048 | tf_op jit(solution)/shard_map/ppermute | solution.py:12
  46.6 7.6 %scatter_custom_fusion = f32[640,512]{1,0:T(8,128)S(1)} fusion(f32[640,512]{1,0:T(8,128)S(1)} %slice_convert_fusion, s32[640]{0:T(1024)} %get-tuple-element.8, bf16[640,512]{1,0:T(8,128)(2,1)S(1)} %fusion.3), kind=kCustom, calls=%fused_computation.27 | custom fusion | flops 655360 | bytes 1966080 | tf_op jit(solution)/shard_map/scatter-add | solution.py:87
  54.2 3.0 %scatter_custom_fusion.2 = f32[640,512]{1,0:T(8,128)S(1)} fusion(s32[320]{0:T(512)S(1)} %compare_select_fusion.6, bf16[320,512]{1,0:T(8,128)(2,1)S(1)} %collective-permute-done.4, f32[]{:T(128)} %constant.14.clone.1), kind=kCustom, calls=%fused_computation.37 | custom fusion | flops 327680 | bytes 1638404 | tf_op jit(solution)/shard_map/scatter-add | solution.py:102
  59.2 10.8 %all-to-all-start.1 = ((bf16[32,8,512]{2,1,0:T(8,128)(2,1)}), bf16[32,8,512]{2,1,0:T(8,128)(2,1)}, u32[]{:S(2)}, u32[]{:S(2)}) async-start(bf16[32,8,512]{2,1,0:T(8,128)(2,1)} %broadcast_in_dim.99), calls=%async_computation.1 | async-start | bytes 524288 | tf_op jit(solution)/shard_map/all_to_all | solution.py:17
  71.8 5.8 %collective-permute-start.6 = (s32[320]{0:T(512)S(1)}, s32[320]{0:T(512)S(1)}, u32[]{:S(2)}, u32[]{:S(2)}) collective-permute-start(s32[320]{0:T(512)S(1)} %broadcast_add_fusion), channel_id=1, source_target_pairs={{0,64},{32,96},{64,0},{96,32},{128,192},{160,224},{192,128},{224,1... | collective-permute-start | bytes 3848 | tf_op jit(solution)/shard_map/ppermute | solution.py:12
  77.6 1.9 %collective-permute-start = (bf16[128,256]{1,0:T(8,128)(2,1)}, bf16[128,256]{1,0:T(8,128)(2,1)}, u32[]{:S(2)}, u32[]{:S(2)}) collective-permute-start(bf16[128,256]{1,0:T(8,128)(2,1)} %param.14), channel_id=1, source_target_pairs={{0,32},{32,0},{64,96},{96,64},{128,160},{160,128},{192,224},{224,1... | collective-permute-start | bytes 196616 | tf_op jit(solution)/shard_map/ppermute | solution.py:12
  79.5 4.0 %all-to-all-done.1 = bf16[32,8,512]{2,1,0:T(8,128)(2,1)} async-done(((bf16[32,8,512]{2,1,0:T(8,128)(2,1)}), bf16[32,8,512]{2,1,0:T(8,128)(2,1)}, u32[]{:S(2)}, u32[]{:S(2)}) %all-to-all-start.1) | async-done | bytes 262176 | tf_op jit(solution)/shard_map/all_to_all | solution.py:17
  87.7 5.8 %collective-permute-start.1 = (bf16[256,256]{1,0:T(8,128)(2,1)S(1)}, bf16[256,256]{1,0:T(8,128)(2,1)S(1)}, u32[]{:S(2)}, u32[]{:S(2)}) collective-permute-start(bf16[256,256]{1,0:T(8,128)(2,1)S(1)} %maximum_select_fusion.7), channel_id=1, source_target_pairs={{0,64},{32,96},{64,0},{96,32},{128,192},{160,224},{192,128},{224,1... | collective-permute-start | bytes 393224 | tf_op jit(solution)/shard_map/ppermute | solution.py:12
  93.6 1.9 %fusion.4 = bf16[640,512]{1,0:T(8,128)(2,1)S(1)} fusion(bf16[640,1024]{1,0:T(8,128)(2,1)} %param.10, pred[640]{0:T(1024)(128)(4,1)} %iota_compare_fusion.1, bf16[256,512]{1,0:T(8,128)(2,1)} %collective-permute-done.5, bf16[256,512]{1,0:T(8,128)(2,1)} %bitcast.15, pred[]{:T(512)S(6)} %eq.5, bf16[640,512]{1,0:T(8,128)(2,1)S(1)} %copy.23), kind=kOutput, calls=%fused_computation.17 | convolution fusion | flops 339542016 | bytes 2492417 | tf_op jit(solution)/shard_map/dot_general | solution.py:71
  95.5 2.0 %gather_fusion.3 = bf16[320,512]{1,0:T(8,128)(2,1)S(1)} fusion(bf16[640,512]{1,0:T(8,128)(2,1)S(1)} %fusion.4, s32[1024]{0:T(1024)S(1)} %pad_clamp_fusion), kind=kCustom, calls=%fused_computation.3 | custom fusion | bytes 656640 | tf_op jit(solution)/shard_map/gather | solution.py:96
  97.5 4.3 %collective-permute-start.7 = (bf16[320,512]{1,0:T(8,128)(2,1)S(1)}, bf16[320,512]{1,0:T(8,128)(2,1)}, u32[]{:S(2)}, u32[]{:S(2)}) collective-permute-start(bf16[320,512]{1,0:T(8,128)(2,1)S(1)} %gather_fusion.3), channel_id=1, source_target_pairs={{0,64},{32,96},{64,0},{96,32},{128,192},{160,224},{192,128},{224,1... | collective-permute-start | bytes 983048 | tf_op jit(solution)/shard_map/ppermute | solution.py:12
  102.0 7.4 %scatter_custom_fusion.3 = f32[640,512]{1,0:T(8,128)S(1)} fusion(f32[640,512]{1,0:T(8,128)S(1)} %slice_convert_fusion.1, s32[640]{0:T(1024)S(1)} %get-tuple-element.6, bf16[640,512]{1,0:T(8,128)(2,1)S(1)} %fusion.4), kind=kCustom, calls=%fused_computation.23 | custom fusion | flops 655360 | bytes 1966080 | tf_op jit(solution)/shard_map/scatter-add | solution.py:87
  109.4 6.4 %collective-permute-done.7 = bf16[320,512]{1,0:T(8,128)(2,1)} collective-permute-done((bf16[320,512]{1,0:T(8,128)(2,1)S(1)}, bf16[320,512]{1,0:T(8,128)(2,1)}, u32[]{:S(2)}, u32[]{:S(2)}) %collective-permute-start.7) | collective-permute-done | bytes 327712 | tf_op jit(solution)/shard_map/ppermute | solution.py:12
  115.9 3.2 %scatter_custom_fusion.5 = f32[640,512]{1,0:T(8,128)S(1)} fusion(s32[320]{0:T(512)S(1)} %compare_select_fusion.4, bf16[320,512]{1,0:T(8,128)(2,1)} %collective-permute-done.7, f32[]{:T(128)} %constant.14.clone.1), kind=kCustom, calls=%fused_computation.35 | custom fusion | flops 327680 | bytes 1638404 | tf_op jit(solution)/shard_map/scatter-add | solution.py:102
  120.4 17.1 %all_to_all.15 = bf16[32,4,512]{2,1,0:T(4,128)(2,1)S(1)} all-to-all(bf16[32,4,512]{2,1,0:T(4,128)(2,1)S(1)} %broadcast_in_dim.103), channel_id=1, replica_groups=mesh['sub'=16,'inner'=32] {'inner'}, dimensions={0} | all-to-all | bytes 262144 | tf_op jit(solution)/shard_map/all_to_all | solution.py:17
  139.5 3.8 %collective-permute-done.8 = bf16[128,512]{1,0:T(8,128)(2,1)S(1)} collective-permute-done((bf16[128,512]{1,0:T(8,128)(2,1)S(1)}, bf16[128,512]{1,0:T(8,128)(2,1)S(1)}, u32[]{:S(2)}, u32[]{:S(2)}) %collective-permute-start.8) | collective-permute-done | bytes 131104 | tf_op jit(solution)/shard_map/ppermute | solution.py:12
  143.3 2.8 %collective-permute-start.9 = (bf16[256,512]{1,0:T(8,128)(2,1)S(1)}, bf16[256,512]{1,0:T(8,128)(2,1)S(1)}, u32[]{:S(2)}, u32[]{:S(2)}) collective-permute-start(bf16[256,512]{1,0:T(8,128)(2,1)S(1)} %maximum_select_fusion.6), channel_id=1, source_target_pairs={{0,64},{32,96},{64,0},{96,32},{128,192},{160,224},{192,128},{224,1... | collective-permute-start | bytes 786440 | tf_op jit(solution)/shard_map/ppermute | solution.py:12
  146.2 13.5 %collective-permute-done.9 = bf16[256,512]{1,0:T(8,128)(2,1)S(1)} collective-permute-done((bf16[256,512]{1,0:T(8,128)(2,1)S(1)}, bf16[256,512]{1,0:T(8,128)(2,1)S(1)}, u32[]{:S(2)}, u32[]{:S(2)}) %collective-permute-start.9) | collective-permute-done | bytes 262176 | tf_op jit(solution)/shard_map/ppermute | solution.py:12
  (88 shorter events, 28.3 us)
Async XLA Ops:
  0.0 2.4 %copy-start = (bf16[512,256]{1,0:T(8,128)(2,1)S(1)}, bf16[512,256]{1,0:T(8,128)(2,1)}, u32[]{:S(2)}) copy-start(bf16[512,256]{1,0:T(8,128)(2,1)} %param.12) | copy-start | bytes 786436
  0.0 2.1 %slice-start = ((bf16[640,1024]{1,0:T(8,128)(2,1)}), bf16[640,512]{1,0:T(8,128)(2,1)S(1)}, s32[]{:S(2)}) async-start(bf16[640,1024]{1,0:T(8,128)(2,1)} %param.9), calls=%async_computation.3 | async-start | bytes 1310720 | tf_op jit(solution)/shard_map/slice | solution.py:58
  2.1 0.5 copy-start.7
  3.8 12.3 %copy-start.1 = (s32[640]{0:T(1024)S(1)}, s32[640]{0:T(1024)}, u32[]{:S(2)}) copy-start(s32[640]{0:T(1024)} %param.16) | copy-start | bytes 7684
  4.9 31.8 %all-to-all-start = ((bf16[32,16,512]{2,1,0:T(8,128)(2,1)}), bf16[32,16,512]{2,1,0:T(8,128)(2,1)S(1)}, u32[]{:S(2)}, u32[]{:S(2)}) async-start(bf16[32,16,512]{2,1,0:T(8,128)(2,1)} %broadcast_in_dim.94), calls=%async_computation | async-start | bytes 1048576 | tf_op jit(solution)/shard_map/all_to_all | solution.py:17
  16.1 13.4 %copy-start.2 = (s32[640]{0:T(1024)S(1)}, s32[640]{0:T(1024)}, u32[]{:S(2)}) copy-start(s32[640]{0:T(1024)} %param.17) | copy-start | bytes 7684
  23.0 14.5 %copy-start.3 = (bf16[640,1024]{1,0:T(8,128)(2,1)S(1)}, bf16[640,1024]{1,0:T(8,128)(2,1)}, u32[]{:S(2)}) copy-start(bf16[640,1024]{1,0:T(8,128)(2,1)} %param.9) | copy-start | bytes 3932164
  23.6 21.2 %collective-permute-start.3 = (s32[320]{0:T(512)}, s32[320]{0:T(512)}, u32[]{:S(2)}, u32[]{:S(2)}) collective-permute-start(s32[320]{0:T(512)} %broadcast_add_fusion.1), channel_id=1, source_target_pairs={{0,32},{32,0},{64,96},{96,64},{128,160},{160,128},{192,224},{224,1... | collective-permute-start | bytes 3848 | tf_op jit(solution)/shard_map/ppermute | solution.py:12
  27.6 17.8 %collective-permute-start.2 = (bf16[256,256]{1,0:T(8,128)(2,1)}, bf16[256,256]{1,0:T(8,128)(2,1)}, u32[]{:S(2)}, u32[]{:S(2)}) collective-permute-start(bf16[256,256]{1,0:T(8,128)(2,1)} %param.13), channel_id=1, source_target_pairs={{0,32},{32,0},{64,96},{96,64},{128,160},{160,128},{192,224},{224,1... | collective-permute-start | bytes 393224 | tf_op jit(solution)/shard_map/ppermute | solution.py:12
  36.7 0.8 copy-start.4
  41.4 12.8 %collective-permute-start.4 = (bf16[320,512]{1,0:T(8,128)(2,1)S(1)}, bf16[320,512]{1,0:T(8,128)(2,1)S(1)}, u32[]{:S(2)}, u32[]{:S(2)}) collective-permute-start(bf16[320,512]{1,0:T(8,128)(2,1)S(1)} %gather_fusion.1), channel_id=1, source_target_pairs={{0,32},{32,0},{64,96},{96,64},{128,160},{160,128},{192,224},{224,1... | collective-permute-start | bytes 983048 | tf_op jit(solution)/shard_map/ppermute | solution.py:12
  57.5 0.7 copy-start.8
  59.2 26.2 %copy-start.5 = (bf16[640,1024]{1,0:T(8,128)(2,1)S(1)}, bf16[640,1024]{1,0:T(8,128)(2,1)}, u32[]{:S(2)}) copy-start(bf16[640,1024]{1,0:T(8,128)(2,1)} %param.11) | copy-start | bytes 3932164
  59.2 24.3 %all-to-all-start.1 = ((bf16[32,8,512]{2,1,0:T(8,128)(2,1)}), bf16[32,8,512]{2,1,0:T(8,128)(2,1)}, u32[]{:S(2)}, u32[]{:S(2)}) async-start(bf16[32,8,512]{2,1,0:T(8,128)(2,1)} %broadcast_in_dim.99), calls=%async_computation.1 | async-start | bytes 524288 | tf_op jit(solution)/shard_map/all_to_all | solution.py:17
  71.8 30.0 %collective-permute-start.6 = (s32[320]{0:T(512)S(1)}, s32[320]{0:T(512)S(1)}, u32[]{:S(2)}, u32[]{:S(2)}) collective-permute-start(s32[320]{0:T(512)S(1)} %broadcast_add_fusion), channel_id=1, source_target_pairs={{0,64},{32,96},{64,0},{96,32},{128,192},{160,224},{192,128},{224,1... | collective-permute-start | bytes 3848 | tf_op jit(solution)/shard_map/ppermute | solution.py:12
  77.6 9.2 %collective-permute-start = (bf16[128,256]{1,0:T(8,128)(2,1)}, bf16[128,256]{1,0:T(8,128)(2,1)}, u32[]{:S(2)}, u32[]{:S(2)}) collective-permute-start(bf16[128,256]{1,0:T(8,128)(2,1)} %param.14), channel_id=1, source_target_pairs={{0,32},{32,0},{64,96},{96,64},{128,160},{160,128},{192,224},{224,1... | collective-permute-start | bytes 196616 | tf_op jit(solution)/shard_map/ppermute | solution.py:12
  83.5 10.0 %collective-permute-start.5 = (bf16[256,512]{1,0:T(8,128)(2,1)}, bf16[256,512]{1,0:T(8,128)(2,1)}, u32[]{:S(2)}, u32[]{:S(2)}) collective-permute-start(bf16[256,512]{1,0:T(8,128)(2,1)} %bitcast.15), channel_id=1, source_target_pairs={{0,32},{32,0},{64,96},{96,64},{128,160},{160,128},{192,224},{224,1... | collective-permute-start | bytes 786440 | tf_op jit(solution)/shard_map/ppermute | solution.py:12
  87.7 14.1 %collective-permute-start.1 = (bf16[256,256]{1,0:T(8,128)(2,1)S(1)}, bf16[256,256]{1,0:T(8,128)(2,1)S(1)}, u32[]{:S(2)}, u32[]{:S(2)}) collective-permute-start(bf16[256,256]{1,0:T(8,128)(2,1)S(1)} %maximum_select_fusion.7), channel_id=1, source_target_pairs={{0,64},{32,96},{64,0},{96,32},{128,192},{160,224},{192,128},{224,1... | collective-permute-start | bytes 393224 | tf_op jit(solution)/shard_map/ppermute | solution.py:12
  97.5 18.3 %collective-permute-start.7 = (bf16[320,512]{1,0:T(8,128)(2,1)S(1)}, bf16[320,512]{1,0:T(8,128)(2,1)}, u32[]{:S(2)}, u32[]{:S(2)}) collective-permute-start(bf16[320,512]{1,0:T(8,128)(2,1)S(1)} %gather_fusion.3), channel_id=1, source_target_pairs={{0,64},{32,96},{64,0},{96,32},{128,192},{160,224},{192,128},{224,1... | collective-permute-start | bytes 983048 | tf_op jit(solution)/shard_map/ppermute | solution.py:12
  119.5 0.7 copy-start.9
  120.1 39.5 %copy-start.6 = (bf16[640,1024]{1,0:T(8,128)(2,1)S(1)}, bf16[640,1024]{1,0:T(8,128)(2,1)}, u32[]{:S(2)}) copy-start(bf16[640,1024]{1,0:T(8,128)(2,1)} %param.11) | copy-start | bytes 3932164
  137.6 5.7 %collective-permute-start.8 = (bf16[128,512]{1,0:T(8,128)(2,1)S(1)}, bf16[128,512]{1,0:T(8,128)(2,1)S(1)}, u32[]{:S(2)}, u32[]{:S(2)}) collective-permute-start(bf16[128,512]{1,0:T(8,128)(2,1)S(1)} %reshape.111), channel_id=1, source_target_pairs={{0,32},{32,0},{64,96},{96,64},{128,160},{160,128},{192,224},{224,1... | collective-permute-start | bytes 393224 | tf_op jit(solution)/shard_map/ppermute | solution.py:12
  143.3 16.3 %collective-permute-start.9 = (bf16[256,512]{1,0:T(8,128)(2,1)S(1)}, bf16[256,512]{1,0:T(8,128)(2,1)S(1)}, u32[]{:S(2)}, u32[]{:S(2)}) collective-permute-start(bf16[256,512]{1,0:T(8,128)(2,1)S(1)} %maximum_select_fusion.6), channel_id=1, source_target_pairs={{0,64},{32,96},{64,0},{96,32},{128,192},{160,224},{192,128},{224,1... | collective-permute-start | bytes 786440 | tf_op jit(solution)/shard_map/ppermute | solution.py:12
where the time goes:
time: 162 us; the launch traced here: 161 us
  starting transfers between devices  55.8 us (34%)
  other arithmetic  31.7 us (20%)
  waiting for transfers between devices  27.7 us (17%)
  local copies, waits for them, and re-layouts  21 us (13%)
  blocking collectives  17.1 us (11%)
  matrix products  7.2 us (4%)
    ppermute x10, starting transfers between devices, swapped(): lax.ppermute(value, axis, [(i, i ^ 1 << bit) for i in range(lax.axis_size...  33.7 us
    ppermute x10, waiting for transfers between devices, swapped(): lax.ppermute(value, axis, [(i, i ^ 1 << bit) for i in range(lax.axis_size...  23.7 us
    all_to_all x2, starting transfers between devices, sent_to_all(): lax.all_to_all(jnp.broadcast_to(value[None], (count, *value.shape)), axis...  22.1 us
    all_to_all x1, blocking collectives, sent_to_all(): lax.all_to_all(jnp.broadcast_to(value[None], (count, *value.shape)), axis...  17.1 us
    scatter-add x2, other arithmetic, extend_add(): own_sum = jnp.zeros((row_count, col_count), jnp.float32).at[own_index].ad...  15 us
    scatter x2, local copies, waits for them, and re-layouts, extend_add(): picked = jnp.zeros((half_rows,), jnp.int32).at[target_slot].set(lax.iota(...  8.16 us
    scatter-add x2, other arithmetic, extend_add(): far_sum = jnp.zeros((row_count, col_count), jnp.float32).at[got_target].a...  6.25 us
    dot_general x3, matrix products, factor_level(): lax.dot_general(factor, pivots, (((1,), (1,)), ((), ())), preferred_eleme...  5.19 us
  transfers between devices with their start and end apart: 12, of which 4 were waited for; matrix products, arithmetic and copies ran while one was open for 27% of the time, Pallas kernels for 0%

commit v1 on v0

v1 whole, which is shorter than its diff:
```python
import jax
import jax.numpy as jnp
from jax import lax
from jax.experimental import pallas as pl
from jax.experimental.pallas import tpu as pltpu
from jax.sharding import PartitionSpec as P

ROWS = 640
PANEL = 512
BLOCK = 256
HALF = ROWS // 2
TILE = 16
INNER = 32
F32 = jnp.float32
BF16 = jnp.bfloat16
MESH = pl.DeviceIdType.MESH

AWAY = (0, 1, -1, 2, -2, 3, -3, 4)
FAR_FIRST = (4, 3, -3, 2, -2, 1, -1)
SLOT = {d: i for i, d in enumerate(AWAY)}
BACK = {d: SLOT[-d] if -d in SLOT else SLOT[d] for d in AWAY}
CHUNKS = ((0, 176), (176, 160), (336, 160), (496, 160))
OWN_CHUNKS = ((16, 160), (176, 160))
FAR_CHUNKS = ((336, 160), (496, 160))


def mm(a, b):
    return lax.dot_general(a, b, (((1,), (0,)), ((), ())), preferred_element_type=F32)


def mmt(a, b):
    return lax.dot_general(a, b, (((1,), (1,)), ((), ())), preferred_element_type=F32)


def iota(shape, dim):
    return lax.broadcasted_iota(jnp.int32, shape, dim)


def hot(cond):
    return jnp.where(cond, 1.0, 0.0).astype(BF16)


def factor_of(panel, inv):
    return jnp.concatenate(
        [mmt(panel[:, b * BLOCK : (b + 1) * BLOCK], inv[b * BLOCK : (b + 1) * BLOCK, :]) for b in range(2)], 1
    ).astype(BF16)


def columns_of(row):
    return jnp.broadcast_to(row, (128, ROWS)).T


def body(
    leaf_hbm, mid_hbm, top_hbm, dinv0, dinv1, dinv2, live, map0, map1, out,
    head, leaf, mid, top, d1, d2, s0, s1, f0, f1, t1, fs, ms, fac, fac1, fac2,
    g, piv, perm, x0, x1, y0, y1, pm, pt, codes, local_sem, send_sem, recv_sem, g_send, g_recv,
):
    s = lax.axis_index("sub")
    j = lax.axis_index("inner")
    bit0 = lax.rem(s, 2)
    bit1 = lax.rem(lax.div(s, 2), 2)
    xh = lax.div(j, 16)
    y = lax.rem(lax.div(j, 2), 8)
    c = lax.rem(j, 2)
    near1 = s + 1 - 2 * bit0
    near2 = s + 2 - 4 * bit1
    near3 = near1 + 2 - 4 * bit1

    def inner(flip_x, dist, flip_c):
        xs = 1 - xh if flip_x else xh
        cs = 1 - c if flip_c else c
        return (s, xs * 16 + lax.rem(y + dist + 8, 8) * 2 + cs)

    def subs(flip):
        return ((s, near1, near2, near3)[flip], j)

    copies = [
        pltpu.make_async_copy(leaf_hbm.at[pl.ds(0, TILE), pl.ds(0, PANEL)], head, local_sem.at[0]),
        pltpu.make_async_copy(leaf_hbm, leaf, local_sem.at[1]),
        pltpu.make_async_copy(mid_hbm, mid, local_sem.at[2]),
        pltpu.make_async_copy(top_hbm, top, local_sem.at[3]),
    ]
    for copy in copies:
        copy.start()

    barrier = pltpu.get_barrier_semaphore()
    partners = [inner(0, d, 0) for d in FAR_FIRST] + [inner(1, d, 0) for d in AWAY] + [inner(0, 0, 1)]
    partners += [subs(f) for f in (1, 2, 3)]
    for partner in partners:
        pl.semaphore_signal(barrier, inc=1, device_id=partner, device_id_type=MESH)

    copies[0].wait()
    g[0, pl.ds(0, TILE)] = factor_of(head[...], dinv0)
    pl.semaphore_wait(barrier, len(partners))

    sends = []

    def send(src, dst, sem, target):
        copy = pltpu.make_async_remote_copy(
            src_ref=src, dst_ref=dst, send_sem=send_sem.at[len(sends)], recv_sem=recv_sem.at[sem],
            device_id=target, device_id_type=MESH,
        )
        copy.start()
        sends.append(copy)

    def arrived(ref, sem):
        pltpu.make_async_remote_copy(
            src_ref=ref, dst_ref=ref, send_sem=send_sem.at[0], recv_sem=sem, device_id=subs(1), device_id_type=MESH
        ).wait_recv()

    def g_copy(lvl, src, dst, sem, target):
        pltpu.make_async_remote_copy(
            src_ref=src, dst_ref=dst, send_sem=g_send.at[lvl], recv_sem=g_recv.at[lvl, sem],
            device_id=target, device_id_type=MESH,
        ).start()

    def gather_start(lvl):
        own = g.at[lvl, pl.ds(0, TILE)]
        for d in FAR_FIRST:
            g_copy(lvl, own, g.at[lvl, pl.ds(128 + BACK[d] * TILE, TILE)], 1, inner(1, d, 0))
            g_copy(lvl, own, g.at[lvl, pl.ds(BACK[d] * TILE, TILE)], 0, inner(0, d, 0))
        g_copy(lvl, own, g.at[lvl, pl.ds(128, TILE)], 1, inner(1, 0, 0))

    def gather_near(lvl):
        arrived(g.at[lvl, pl.ds(TILE, 112)], g_recv.at[lvl, 0])
        g_copy(lvl, g.at[lvl, pl.ds(0, 128)], g.at[lvl, pl.ds(256, 128)], 2, inner(0, 0, 1))

    def gather_far(lvl):
        arrived(g.at[lvl, pl.ds(128, 128)], g_recv.at[lvl, 1])
        g_copy(lvl, g.at[lvl, pl.ds(128, 128)], g.at[lvl, pl.ds(384, 128)], 3, inner(0, 0, 1))

    def gather_end(lvl):
        arrived(g.at[lvl, pl.ds(256, 128)], g_recv.at[lvl, 2])
        arrived(g.at[lvl, pl.ds(384, 128)], g_recv.at[lvl, 3])
        piv[...] = mm(perm[lvl], g[lvl]).astype(BF16)

    gather_start(0)
    send(dinv1, d1.at[pl.ds(pl.multiple_of(bit0 * 256, 256), 256)], 0, subs(1))
    quarter = pl.ds(pl.multiple_of((bit0 + 2 * bit1) * 128, 128), 128)
    for f in (1, 2, 3):
        send(dinv2, d2.at[quarter], f, subs(f))
    copies[2].wait()
    send(mid.at[pl.ds(0, TILE), pl.ds(0, PANEL)], pm.at[pl.ds(48, TILE)], 4, subs(1))
    copies[3].wait()
    for f in (1, 2, 3):
        send(top.at[pl.ds(0, TILE), pl.ds(0, PANEL)], pt.at[pl.ds(64 + 16 * f, TILE)], 4 + f, subs(f))

    def order(codes_row):
        down = columns_of(codes_row)[:, 0:1]
        rank = jnp.sum(jnp.where(down < codes_row, 1.0, 0.0), axis=0, keepdims=True)
        rank_down = columns_of(rank)[:, 0:1]
        at = iota((ROWS, ROWS), 1).astype(F32)
        return rank, jnp.sum(jnp.where(rank_down == at, down, 0.0), axis=0, keepdims=True)

    e0 = map0[...].astype(F32)
    e1 = map1[...].astype(F32)
    rank0, sorted0 = order(e0)
    codes[0] = jnp.broadcast_to(sorted0, (8, ROWS))
    send(codes.at[0], codes.at[1], 8, subs(1))
    rank1, sorted1 = order(e1)
    codes[2] = jnp.broadcast_to(sorted1, (8, ROWS))
    send(codes.at[2], codes.at[3], 9, subs(2))

    lanes = iota((1, ROWS), 1)
    live_f = live[...]

    def ordering(ref, codes_row, rank, early, level):
        alive = lanes < live_f[:, level : level + 1]
        slot = iota((TILE, ROWS), 0)
        wanted = jnp.where(slot < early, slot, jnp.where(slot < 2 * early, ROWS - early + slot, -1)).astype(F32)
        ref[pl.ds(0, TILE)] = hot((codes_row == wanted) & alive)
        for r, n in ((16, 160), (176, 160), (336, 160), (496, 160)):
            ref[pl.ds(r, n)] = hot((rank == (iota((n, ROWS), 0) + (r - TILE)).astype(F32)) & alive)

    ordering(s0, e0, rank0, 8, 0)
    copies[1].wait()
    for r, n in CHUNKS:
        for h in range(2):
            part = pl.ds(h * PANEL, PANEL)
            fs[pl.ds(r, n), part] = mm(s0[pl.ds(r, n)], leaf[:, part]).astype(BF16)
    gather_near(0)
    for r, n in CHUNKS:
        fac[pl.ds(r, n)] = factor_of(fs[pl.ds(r, n), pl.ds(0, PANEL)], dinv0)

    q = iota((1, PANEL), 1)
    block = (q >> 4) & 7
    dist = jnp.where(block & 1 == 1, (block + 1) >> 1, -(block >> 1))
    x_from = xh ^ ((q >> 7) & 1)
    y_from = (y + dist + 8) & 7
    j_from = x_from * 16 + y_from * 2 + (c ^ (q >> 8))
    i = q & 15
    targets = (
        j_from * 16 + i,
        (bit0 ^ (i >> 3)) * 256 + j_from * 8 + (i & 7),
        ((bit0 + 2 * bit1) ^ (i >> 2)) * 128 + j_from * 4 + (i & 3),
    )
    down = iota((PANEL, PANEL), 0)
    for lvl in range(3):
        perm[lvl] = hot(targets[lvl] == down)
    gather_far(0)

    def landing(ref, mine, far, sem, live_rows):
        arrived(codes.at[far], recv_sem.at[sem])
        at = jnp.where(lanes < HALF, codes[mine, 0:1, :], codes[far, 0:1, :] - ROWS)
        for r in range(0, ROWS, 160):
            row = iota((160, ROWS), 0) + r
            hit = row.astype(F32) == at
            if live_rows is not None:
                hit = hit & (row < live_rows)
            ref[pl.ds(r, 160)] = hot(hit)

    landing(f0, 0, 1, 8, None)
    ordering(s1, e1, rank1, 4, 1)
    for r, n in CHUNKS:
        for h in range(2):
            part = pl.ds(h * PANEL, PANEL)
            ms[pl.ds(r, n), part] = mm(s1[pl.ds(r, n)], mid[:, part]).astype(BF16)
    gather_end(0)

    def update(front, factor, rows):
        product = mmt(factor[rows], piv[...])
        return (front[rows, pl.ds(PANEL, PANEL)].astype(F32) - product).astype(BF16)

    def far_updates(front, factor, store, other, sem, flip):
        for k, (r, n) in enumerate(FAR_CHUNKS):
            store[pl.ds(k * 160, n)] = update(front, factor, pl.ds(r, n))
            send(store.at[pl.ds(k * 160, n)], other.at[pl.ds(HALF + k * 160, n)], sem + k, subs(flip))

    def own_updates(front, factor, other):
        for r, n in OWN_CHUNKS:
            other[pl.ds(r - TILE, n)] = update(front, factor, pl.ds(r, n))

    def one_of(rows, width, *columns):
        i = iota((rows, width), 0)
        k = iota((rows, width), 1)
        hit = k == columns[0](i)
        for column in columns[1:]:
            hit = hit | (k == column(i))
        return hot(hit)

    pm[pl.ds(0, TILE)] = update(fs, fac, pl.ds(0, TILE))
    send(pm.at[pl.ds(0, TILE)], pm.at[pl.ds(16, TILE)], 10, subs(1))
    far_updates(fs, fac, y0, x0, 11, 1)
    pm[pl.ds(32, TILE)] = mid[pl.ds(0, TILE), pl.ds(0, PANEL)]
    d1[pl.ds(pl.multiple_of(bit0 * 256, 256), 256)] = dinv1[...]
    arrived(d1.at[pl.ds(pl.multiple_of((1 - bit0) * 256, 256), 256)], recv_sem.at[0])
    arrived(pm.at[pl.ds(48, TILE)], recv_sem.at[4])
    arrived(pm.at[pl.ds(16, TILE)], recv_sem.at[10])
    pick1 = one_of(
        TILE, 64, lambda i: i, lambda i: jnp.where(i < 8, i + 24, i + 8), lambda i: jnp.where(i < 8, i + 32, i + 40)
    )
    g[1, pl.ds(0, TILE)] = factor_of(mm(pick1, pm[...]).astype(BF16), d1)
    gather_start(1)
    own_updates(fs, fac, x0)
    for r, n in CHUNKS:
        t1[pl.ds(r, n)] = mm(s1[pl.ds(r, n)], f0[...]).astype(BF16)
    gather_near(1)
    for k in range(2):
        arrived(x0.at[pl.ds(HALF + k * 160, 160)], recv_sem.at[11 + k])
    for r, n in CHUNKS:
        rows = pl.ds(r, n)
        whole = (ms[rows, pl.ds(0, PANEL)].astype(F32) + mm(t1[rows], x0[...])).astype(BF16)
        fac1[rows] = factor_of(whole, d1)
    gather_far(1)
    gather_end(1)

    pt[pl.ds(0, TILE)] = update(ms, fac1, pl.ds(0, TILE))
    for f in (1, 2, 3):
        send(pt.at[pl.ds(0, TILE)], pt.at[pl.ds(16 * f, TILE)], 12 + f, subs(f))
    far_updates(ms, fac1, y1, x1, 16, 2)
    pt[pl.ds(64, TILE)] = top[pl.ds(0, TILE), pl.ds(0, PANEL)]
    d2[quarter] = dinv2[...]
    for f in (1, 2, 3):
        theirs = ((0, bit0 + 2 * bit1), (1, 1 - bit0 + 2 * bit1), (2, bit0 + 2 - 2 * bit1), (3, 3 - bit0 - 2 * bit1))[f][1]
        arrived(d2.at[pl.ds(pl.multiple_of(theirs * 128, 128), 128)], recv_sem.at[f])
        arrived(pt.at[pl.ds(64 + 16 * f, TILE)], recv_sem.at[4 + f])
        arrived(pt.at[pl.ds(16 * f, TILE)], recv_sem.at[12 + f])
    pick2 = one_of(
        TILE, 128,
        lambda i: (i >> 2) * 16 + (i & 3), lambda i: ((i >> 2) ^ 2) * 16 + 4 + (i & 3), lambda i: 64 + (i >> 2) * 16 + (i & 3),
    )
    g[2, pl.ds(0, TILE)] = factor_of(mm(pick2, pt[...]).astype(BF16), d2)
    gather_start(2)
    own_updates(ms, fac1, x1)
    landing(f1, 2, 3, 9, live_f[:, 2:3])
    gather_near(2)
    for k in range(2):
        arrived(x1.at[pl.ds(HALF + k * 160, 160)], recv_sem.at[16 + k])
    for r in range(0, ROWS, 160):
        rows = pl.ds(r, 160)
        alive = (iota((160, PANEL), 0) + r) < live_f[:, 2:3]
        whole = top[rows, pl.ds(0, PANEL)].astype(F32) + mm(f1[rows], x1[...])
        fac2[rows] = factor_of(jnp.where(alive, whole, 0.0).astype(BF16), d2)
    gather_far(2)
    gather_end(2)

    for r in range(0, ROWS, 160):
        rows = pl.ds(r, 160)
        alive = (iota((160, PANEL), 0) + r) < live_f[:, 2:3]
        product = mmt(fac2[rows], piv[...])
        out[rows] = jnp.where(alive, top[rows, pl.ds(PANEL, PANEL)].astype(F32) - product, 0.0).astype(BF16)

    for copy in sends:
        copy.wait_send()
    for lvl in range(3):
        ref = g.at[lvl, pl.ds(0, 496)]
        pltpu.make_async_remote_copy(
            src_ref=ref, dst_ref=ref, send_sem=g_send.at[lvl], recv_sem=g_recv.at[lvl, 0],
            device_id=subs(1), device_id_type=MESH,
        ).wait_send()


def per_device(leaf, mid, top, dinv0, dinv1, dinv2, live_rows, map0, map1):
    vmem = pl.BlockSpec(memory_space=pltpu.VMEM)
    hbm = pl.BlockSpec(memory_space=pl.ANY)
    held = lambda *shape: pltpu.VMEM(shape, BF16)
    more = ROWS + TILE
    return pl.pallas_call(
        body,
        name="panel_steps",
        out_shape=jax.ShapeDtypeStruct((ROWS, PANEL), BF16),
        in_specs=[hbm] * 3 + [vmem] * 6,
        out_specs=vmem,
        scratch_shapes=[
            held(TILE, PANEL),
            held(ROWS, 1024),
            held(ROWS, 1024),
            held(ROWS, 1024),
            held(PANEL, BLOCK),
            held(PANEL, BLOCK),
            held(more, ROWS),
            held(more, ROWS),
            held(ROWS, ROWS),
            held(ROWS, ROWS),
            held(more, ROWS),
            held(more, 1024),
            held(more, 1024),
            held(more, PANEL),
            held(more, PANEL),
            held(ROWS, PANEL),
            held(3, PANEL, PANEL),
            held(PANEL, PANEL),
            held(3, PANEL, PANEL),
            held(ROWS, PANEL),
            held(ROWS, PANEL),
            held(HALF, PANEL),
            held(HALF, PANEL),
            held(64, PANEL),
            held(128, PANEL),
            pltpu.VMEM((4, 8, ROWS), F32),
            pltpu.SemaphoreType.DMA((4,)),
            pltpu.SemaphoreType.DMA((24,)),
            pltpu.SemaphoreType.DMA((18,)),
            pltpu.SemaphoreType.DMA((3,)),
            pltpu.SemaphoreType.DMA((3, 4)),
        ],
        compiler_params=pltpu.CompilerParams(
            collective_id=0, has_side_effects=True, vmem_limit_bytes=48 * 2**20
        ),
    )(leaf, mid, top, dinv0, dinv1, dinv2, live_rows.reshape(1, 3), map0.reshape(1, ROWS), map1.reshape(1, ROWS))


def solution(mesh):
    rows = P(("sub", "inner"), None)
    placed = (
        rows, rows, rows, P("sub", None), P("sub", None), P("sub", None),
        P(None, ("sub", "inner")), P(("sub", "inner")), P(("sub", "inner")),
    )
    return jax.shard_map(per_device, mesh=mesh, in_specs=placed, out_specs=rows, check_vma=False)
```

time: 162 us -> 69.1 us (0.43)
  Pallas kernels: 0 us -> 59.2 us
  starting transfers between devices: 55.8 us -> 0 us
  other arithmetic: 31.7 us -> 0 us
  waiting for transfers between devices: 27.7 us -> 0 us
  blocking collectives: 17.1 us -> 0 us
  local copies, waits for them, and re-layouts: 21 us -> 9.51 us
  matrix products: 7.2 us -> 0 us
    pallas_call x0 -> x1, Pallas kernels: none -> 59.2 us  [per_device(): pl.pallas_call(body, name='panel_steps', out_shape=jax.ShapeDtypeStruct((...]
    ppermute x10 -> x0, starting transfers between devices: 33.7 us -> none  [swapped(): lax.ppermute(value, axis, [(i, i ^ 1 << bit) for i in range(lax.axis_size...]
    ppermute x10 -> x0, waiting for transfers between devices: 23.7 us -> none  [swapped(): lax.ppermute(value, axis, [(i, i ^ 1 << bit) for i in range(lax.axis_size...]
    all_to_all x2 -> x0, starting transfers between devices: 22.1 us -> none  [sent_to_all(): lax.all_to_all(jnp.broadcast_to(value[None], (count, *value.shape)), axis...]
    scatter-add x4 -> x0, other arithmetic: 21.3 us -> none  [the longest x2 15 us: extend_add(): own_sum = jnp.zeros((row_count, col_count), jnp.float32).at[own_index].ad...]
    all_to_all x1 -> x0, blocking collectives: 17.1 us -> none  [sent_to_all(): lax.all_to_all(jnp.broadcast_to(value[None], (count, *value.shape)), axis...]
    scatter x2 -> x0, local copies, waits for them, and re-layouts: 8.16 us -> none  [extend_add(): picked = jnp.zeros((half_rows,), jnp.int32).at[target_slot].set(lax.iota(...]
    gather x4 -> x0, local copies, waits for them, and re-layouts: 7.42 us -> none  [the longest x2 4.05 us: extend_add(): sent_rows = update[picked]]
  transfers between devices with their start and end apart: 12 -> 0, of which waited for: 4 -> 0; matrix products, arithmetic and copies ran while one was open for 27% -> 0% of each run, Pallas kernels for 0% -> 0%
where the time goes in v1:
time: 69.1 us; the launch traced here: 68.7 us
  Pallas kernels  59.2 us (86%)
  local copies, waits for them, and re-layouts  9.51 us (14%)
    pallas_call x1, Pallas kernels, per_device(): pl.pallas_call(body, name='panel_steps', out_shape=jax.ShapeDtypeStruct((...  59.2 us
    unnamed x15, local copies, waits for them, and re-layouts  8.13 us

profile of v1, /device:TPU:1, one launch (start us, length us, event | category | flops | bytes accessed | tf_op | source)
XLA Modules:
  0.0 68.7 jit_solution(12830962135315622857)
XLA Ops:
  0.0 0.7 %reshape.10.map0 = s32[1,640]{1,0:T(1,128)S(1)} reshape(s32[640]{0:T(1024)} %param.16) | data formatting | bytes 5120 | tf_op jit(solution)/shard_map/reshape | solution.py:360
  0.7 0.7 %reshape.11.map1 = s32[1,640]{1,0:T(1,128)S(1)} reshape(s32[640]{0:T(1024)} %param.17) | data formatting | bytes 5120 | tf_op jit(solution)/shard_map/reshape | solution.py:360
  1.4 0.0 copy-start
  1.4 1.3 %copy-done = bf16[640,1024]{1,0:T(8,128)(2,1)S(1)} copy-done((bf16[640,1024]{1,0:T(8,128)(2,1)S(1)}, bf16[640,1024]{1,0:T(8,128)(2,1)}, u32[]{:S(2)}) %copy-start) | copy-done | bytes 1310744
  2.7 0.0 copy-start.1
  2.7 1.3 %copy-done.1 = bf16[640,1024]{1,0:T(8,128)(2,1)S(1)} copy-done((bf16[640,1024]{1,0:T(8,128)(2,1)S(1)}, bf16[640,1024]{1,0:T(8,128)(2,1)}, u32[]{:S(2)}) %copy-start.1) | copy-done | bytes 1310744
  4.0 0.0 copy-start.2
  4.0 1.3 %copy-done.2 = bf16[640,1024]{1,0:T(8,128)(2,1)S(1)} copy-done((bf16[640,1024]{1,0:T(8,128)(2,1)S(1)}, bf16[640,1024]{1,0:T(8,128)(2,1)}, u32[]{:S(2)}) %copy-start.2) | copy-done | bytes 1310744
  5.3 0.0 copy-start.3
  5.3 0.9 %copy-done.3 = bf16[512,256]{1,0:T(8,128)(2,1)S(1)} copy-done((bf16[512,256]{1,0:T(8,128)(2,1)S(1)}, bf16[512,256]{1,0:T(8,128)(2,1)}, u32[]{:S(2)}) %copy-start.3) | copy-done | bytes 262168
  6.3 0.0 copy-start.4
  6.3 0.9 %copy-done.4 = bf16[256,256]{1,0:T(8,128)(2,1)S(1)} copy-done((bf16[256,256]{1,0:T(8,128)(2,1)S(1)}, bf16[256,256]{1,0:T(8,128)(2,1)}, u32[]{:S(2)}) %copy-start.4) | copy-done | bytes 131096
  7.2 0.0 copy-start.5
  7.2 0.8 %copy-done.5 = bf16[128,256]{1,0:T(8,128)(2,1)S(1)} copy-done((bf16[128,256]{1,0:T(8,128)(2,1)S(1)}, bf16[128,256]{1,0:T(8,128)(2,1)}, u32[]{:S(2)}) %copy-start.5) | copy-done | bytes 65560
  8.0 0.0 copy-start.6
  8.0 0.7 copy-done.6
  8.7 59.2 %panel_steps.1 = bf16[640,512]{1,0:T(8,128)(2,1)S(1)} custom-call(bf16[640,1024]{1,0:T(8,128)(2,1)S(1)} %copy-done, bf16[640,1024]{1,0:T(8,128)(2,1)S(1)} %copy-done.1, bf16[640,1024]{1,0:T(8,128)(2,1)S(1)} %copy-done.2, bf16[512,256]{1,0:T(8,128)(2,1)S(1)} %copy-done.3, bf16[256,256]{1,0:T(8,128)(2,1)S(1)} %copy-done.4, bf16[128,256]{1,0:T(8,128)(2,1)S(1)} %copy-done.5, ...), custom_call_target="tpu_custom_call" | custom-call | tf_op jit(solution)/shard_map/panel_steps/pallas_call | solution.py:318
  67.9 0.8 %copy.11 = bf16[640,512]{1,0:T(8,128)(2,1)} copy(bf16[640,512]{1,0:T(8,128)(2,1)S(1)} %panel_steps.1) | data formatting | bytes 1310720
Async XLA Ops:
  1.4 1.3 %copy-start = (bf16[640,1024]{1,0:T(8,128)(2,1)S(1)}, bf16[640,1024]{1,0:T(8,128)(2,1)}, u32[]{:S(2)}) copy-start(bf16[640,1024]{1,0:T(8,128)(2,1)} %leaf_hbm.1) | copy-start | bytes 3932164
  2.7 1.3 %copy-start.1 = (bf16[640,1024]{1,0:T(8,128)(2,1)S(1)}, bf16[640,1024]{1,0:T(8,128)(2,1)}, u32[]{:S(2)}) copy-start(bf16[640,1024]{1,0:T(8,128)(2,1)} %mid_hbm.1) | copy-start | bytes 3932164
  4.0 1.3 %copy-start.2 = (bf16[640,1024]{1,0:T(8,128)(2,1)S(1)}, bf16[640,1024]{1,0:T(8,128)(2,1)}, u32[]{:S(2)}) copy-start(bf16[640,1024]{1,0:T(8,128)(2,1)} %top_hbm.1) | copy-start | bytes 3932164
  5.3 0.9 %copy-start.3 = (bf16[512,256]{1,0:T(8,128)(2,1)S(1)}, bf16[512,256]{1,0:T(8,128)(2,1)}, u32[]{:S(2)}) copy-start(bf16[512,256]{1,0:T(8,128)(2,1)} %dinv0.1) | copy-start | bytes 786436
  6.3 0.9 %copy-start.4 = (bf16[256,256]{1,0:T(8,128)(2,1)S(1)}, bf16[256,256]{1,0:T(8,128)(2,1)}, u32[]{:S(2)}) copy-start(bf16[256,256]{1,0:T(8,128)(2,1)} %dinv1.1) | copy-start | bytes 393220
  7.2 0.8 %copy-start.5 = (bf16[128,256]{1,0:T(8,128)(2,1)S(1)}, bf16[128,256]{1,0:T(8,128)(2,1)}, u32[]{:S(2)}) copy-start(bf16[128,256]{1,0:T(8,128)(2,1)} %dinv2.1) | copy-start | bytes 196612
  8.0 0.7 copy-start.6

commit v2 on v1

v2 whole, which is shorter than its diff:
```python
import jax
import jax.numpy as jnp
from jax import lax
from jax.experimental import pallas as pl
from jax.experimental.pallas import tpu as pltpu
from jax.sharding import PartitionSpec as P

ROWS = 640
PANEL = 512
BLOCK = 256
HALF = ROWS // 2
TILE = 16
INNER = 32
F32 = jnp.float32
BF16 = jnp.bfloat16
MESH = pl.DeviceIdType.MESH

AWAY = (0, 1, -1, 2, -2, 3, -3, 4)
FAR_FIRST = (4, 3, -3, 2, -2, 1, -1)
SLOT = {d: i for i, d in enumerate(AWAY)}
BACK = {d: SLOT[-d] if -d in SLOT else SLOT[d] for d in AWAY}
CHUNKS = ((0, 336), (336, 320))
OWN_CHUNKS = ((16, 320),)
FAR_CHUNKS = ((336, 192), (528, 128))


def mm(a, b):
    return lax.dot_general(a, b, (((1,), (0,)), ((), ())), preferred_element_type=F32)


def mmt(a, b):
    return lax.dot_general(a, b, (((1,), (1,)), ((), ())), preferred_element_type=F32)


def iota(shape, dim):
    return lax.broadcasted_iota(jnp.int32, shape, dim)


def hot(cond):
    return jnp.where(cond, 1.0, 0.0).astype(BF16)


def factor_of(panel, inv):
    return jnp.concatenate(
        [mmt(panel[:, b * BLOCK : (b + 1) * BLOCK], inv[b * BLOCK : (b + 1) * BLOCK, :]) for b in range(2)], 1
    ).astype(BF16)


def columns_of(row):
    return jnp.broadcast_to(row, (128, ROWS)).T


def body(
    leaf_hbm, mid_hbm, top_hbm, dinv0_hbm, dinv1_hbm, dinv2_hbm, live_hbm, map0_hbm, map1_hbm, out,
    lead, leaf, mid, top, dinv0, live, map0, map1, d1, d2, s0, s1, f0, f1, t1, fs, ms, fac, fac1, fac2,
    g, piv, perm, x0, x1, y0, y1, pm, pt, pick1, pick2, acc, res, codes, local_sem, send_sem, recv_sem, g_send, g_recv,
):
    s = lax.axis_index("sub")
    j = lax.axis_index("inner")
    bit0 = lax.rem(s, 2)
    bit1 = lax.rem(lax.div(s, 2), 2)
    xh = lax.div(j, 16)
    y = lax.rem(lax.div(j, 2), 8)
    c = lax.rem(j, 2)
    near1 = s + 1 - 2 * bit0
    near2 = s + 2 - 4 * bit1
    near3 = near1 + 2 - 4 * bit1

    def inner(flip_x, dist, flip_c):
        xs = 1 - xh if flip_x else xh
        cs = 1 - c if flip_c else c
        return (s, xs * 16 + lax.rem(y + dist + 8, 8) * 2 + cs)

    def subs(flip):
        return ((s, near1, near2, near3)[flip], j)

    copies = [
        pltpu.make_async_copy(leaf_hbm.at[pl.ds(0, TILE), pl.ds(0, PANEL)], lead.at[xh, y, c], local_sem.at[0]),
        pltpu.make_async_copy(dinv0_hbm, dinv0, local_sem.at[1]),
        pltpu.make_async_copy(map0_hbm, map0, local_sem.at[2]),
        pltpu.make_async_copy(map1_hbm, map1, local_sem.at[3]),
        pltpu.make_async_copy(live_hbm, live, local_sem.at[4]),
        pltpu.make_async_copy(leaf_hbm, leaf, local_sem.at[5]),
        pltpu.make_async_copy(mid_hbm, mid, local_sem.at[6]),
        pltpu.make_async_copy(top_hbm, top, local_sem.at[7]),
        pltpu.make_async_copy(dinv1_hbm, d1.at[pl.ds(pl.multiple_of(bit0 * 256, 256), 256)], local_sem.at[8]),
        pltpu.make_async_copy(
            dinv2_hbm, d2.at[pl.ds(pl.multiple_of((bit0 + 2 * bit1) * 128, 128), 128)], local_sem.at[9]
        ),
    ]
    barrier = pltpu.get_barrier_semaphore()
    partners = [inner(0, d, 0) for d in FAR_FIRST] + [inner(1, d, 0) for d in AWAY[:5]] + [inner(1, 0, 1), inner(0, 0, 1)]
    partners += [subs(f) for f in (1, 2, 3)]
    for partner in partners:
        pl.semaphore_signal(barrier, inc=1, device_id=partner, device_id_type=MESH)

    for copy in copies:
        copy.start()
    pl.semaphore_wait(barrier, len(partners))

    sends = []

    def send(src, dst, sem, target):
        copy = pltpu.make_async_remote_copy(
            src_ref=src, dst_ref=dst, send_sem=send_sem.at[len(sends)], recv_sem=recv_sem.at[sem],
            device_id=target, device_id_type=MESH,
        )
        copy.start()
        sends.append(copy)

    def arrived(ref, sem):
        pltpu.make_async_remote_copy(
            src_ref=ref, dst_ref=ref, send_sem=send_sem.at[0], recv_sem=sem, device_id=subs(1), device_id_type=MESH
        ).wait_recv()

    def g_copy(lvl, src, dst, sem, target):
        pltpu.make_async_remote_copy(
            src_ref=src, dst_ref=dst, send_sem=g_send.at[lvl], recv_sem=g_recv.at[lvl, sem],
            device_id=target, device_id_type=MESH,
        ).start()

    def place(lvl, flip_x, d, mine):
        if lvl == 0:
            return lead.at[xh, y, c] if mine else lead.at[1 - xh if flip_x else xh, lax.rem(y + d + 8, 8), c]
        return g.at[lvl - 1, pl.ds(128 * flip_x + (BACK[d] if mine else SLOT[d]) * TILE, TILE)]

    def column(lvl, flip_x, flip_c):
        if lvl == 0:
            return lead.at[1 - xh if flip_x else xh, :, 1 - c if flip_c else c]
        return g.at[lvl - 1, pl.ds(256 * flip_c + 128 * flip_x, 128)]

    def seven(lvl):
        return lead.at[0, pl.ds(0, 7), 0] if lvl == 0 else g.at[lvl - 1, pl.ds(0, 112)]

    def gather_start(lvl, own):
        for d in FAR_FIRST:
            g_copy(lvl, own, place(lvl, 0, d, True), 0, inner(0, d, 0))
        for d in FAR_FIRST[3:] + (0,):
            g_copy(lvl, own, place(lvl, 1, d, True), 1, inner(1, d, 0))

    def y_landed(lvl):
        arrived(seven(lvl), g_recv.at[lvl, 0])
        for d in FAR_FIRST[:3]:
            part = place(lvl, 0, d, False)
            for flip_c in (0, 1):
                to = part if lvl == 0 else g.at[lvl - 1, pl.ds(256 * flip_c + 128 + SLOT[d] * TILE, TILE)]
                g_copy(lvl, part, to, 4 + flip_c, inner(1, 0, flip_c))
        part = column(lvl, 0, 0)
        g_copy(lvl, part, part if lvl == 0 else column(lvl, 0, 1), 2, inner(0, 0, 1))

    def five(lvl):
        return lead.at[0, pl.ds(0, 5), 0] if lvl == 0 else g.at[lvl - 1, pl.ds(128, 80)]

    def three(lvl, flip_c):
        return lead.at[0, pl.ds(0, 3), 0] if lvl == 0 else g.at[lvl - 1, pl.ds(256 * flip_c + 208, 48)]

    def x_landed(lvl):
        arrived(five(lvl), g_recv.at[lvl, 1])
        if lvl == 0:
            for d in (0,) + FAR_FIRST[3:]:
                part = place(0, 1, d, False)
                g_copy(lvl, part, part, 3, inner(0, 0, 1))
        else:
            g_copy(lvl, five(lvl), g.at[lvl - 1, pl.ds(384, 80)], 3, inner(0, 0, 1))

    def gather_end(lvl):
        arrived(three(lvl, 0), g_recv.at[lvl, 4])
        if lvl > 0:
            half = mm(perm[lvl - 1, :, pl.ds(0, 256)], g[lvl - 1, pl.ds(0, 256)])
        arrived(column(lvl, 0, 1), g_recv.at[lvl, 2])
        arrived(five(lvl) if lvl == 0 else g.at[lvl - 1, pl.ds(384, 80)], g_recv.at[lvl, 3])
        arrived(three(lvl, 1), g_recv.at[lvl, 5])
        if lvl > 0:
            half += mm(perm[lvl - 1, :, pl.ds(256, 256)], g[lvl - 1, pl.ds(256, 256)])
            piv[...] = half.astype(BF16)
        else:
            piv[...] = factor_of(lead[...].reshape(PANEL, PANEL), dinv0)

    gather_start(0, leaf_hbm.at[pl.ds(0, TILE), pl.ds(0, PANEL)])
    quarter = pl.ds(pl.multiple_of((bit0 + 2 * bit1) * 128 + c * 64, 64), 64)
    half = pl.ds(pl.multiple_of(bit0 * 256 + c * 128, 128), 128)
    send(dinv1_hbm.at[pl.ds(pl.multiple_of(c * 128, 128), 128)], d1.at[half], 0, subs(1))
    send(mid_hbm.at[pl.ds(0, TILE), pl.ds(0, PANEL)], pm.at[pl.ds(48, TILE)], 4, subs(1))
    for f in (1, 2, 3):
        send(top_hbm.at[pl.ds(0, TILE), pl.ds(0, PANEL)], pt.at[pl.ds(64 + 16 * f, TILE)], 4 + f, subs(f))
        send(dinv2_hbm.at[pl.ds(pl.multiple_of(c * 64, 64), 64)], d2.at[quarter], f, subs(f))

    def order(codes_row):
        down = columns_of(codes_row)[:, 0:1]
        rank = jnp.sum(jnp.where(down < codes_row, 1.0, 0.0), axis=0, keepdims=True)
        rank_down = columns_of(rank)[:, 0:1]
        at = iota((ROWS, ROWS), 1).astype(F32)
        return rank, jnp.sum(jnp.where(rank_down == at, down, 0.0), axis=0, keepdims=True)

    for copy in copies[2:5]:
        copy.wait()
    e0 = map0[...].astype(F32).reshape(1, ROWS)
    e1 = map1[...].astype(F32).reshape(1, ROWS)
    rank0, sorted0 = order(e0)
    codes[0] = jnp.broadcast_to(sorted0, (8, ROWS))
    send(codes.at[0], codes.at[1], 8, subs(1))
    rank1, sorted1 = order(e1)
    codes[2] = jnp.broadcast_to(sorted1, (8, ROWS))
    send(codes.at[2], codes.at[3], 9, subs(2))

    lanes = iota((1, ROWS), 1)
    live_f = live[...]

    def ordering(ref, codes_row, rank, early, level):
        alive = lanes < live_f[:, level : level + 1]
        slot = iota((TILE, ROWS), 0)
        wanted = jnp.where(slot < early, slot, jnp.where(slot < 2 * early, ROWS - early + slot, -1)).astype(F32)
        ref[pl.ds(0, TILE)] = hot((codes_row == wanted) & alive)
        for r, n in ((16, 160), (176, 160), (336, 160), (496, 160)):
            ref[pl.ds(r, n)] = hot((rank == (iota((n, ROWS), 0) + (r - TILE)).astype(F32)) & alive)

    ordering(s0, e0, rank0, 8, 0)
    copies[5].wait()

    def ordered(ref, order_ref, front, chunks):
        for r, n in chunks:
            for h in range(2):
                part = pl.ds(h * PANEL, PANEL)
                ref[pl.ds(r, n), part] = mm(order_ref[pl.ds(r, n)], front[:, part]).astype(BF16)

    ordered(fs, s0, leaf, CHUNKS)
    copies[1].wait()
    for r, n in CHUNKS:
        fac[pl.ds(r, n)] = factor_of(fs[pl.ds(r, n), pl.ds(0, PANEL)], dinv0)
    copies[0].wait()
    y_landed(0)
    got = d1.at[pl.ds(pl.multiple_of((1 - bit0) * 256 + c * 128, 128), 128)]
    arrived(got, recv_sem.at[0])
    send(got, got, 18, inner(0, 0, 1))

    q = iota((1, PANEL), 1)
    block = (q >> 4) & 7
    dist = jnp.where(block & 1 == 1, (block + 1) >> 1, -(block >> 1))
    x_from = xh ^ ((q >> 7) & 1)
    y_from = (y + dist + 8) & 7
    j_from = x_from * 16 + y_from * 2 + (c ^ (q >> 8))
    i = q & 15
    targets = (
        (bit0 ^ (i >> 3)) * 256 + j_from * 8 + (i & 7),
        ((bit0 + 2 * bit1) ^ (i >> 2)) * 128 + j_from * 4 + (i & 3),
    )
    down = iota((PANEL, PANEL), 0)
    for lvl in range(2):
        perm[lvl] = hot(targets[lvl] == down)

    def one_of(ref, *columns):
        i = iota(ref.shape, 0)
        k = iota(ref.shape, 1)
        hit = k == columns[0](i)
        for column in columns[1:]:
            hit = hit | (k == column(i))
        ref[...] = hot(hit)

    one_of(
        pick1, lambda i: i, lambda i: jnp.where(i < 8, i + 24, i + 8), lambda i: jnp.where(i < 8, i + 32, i + 40)
    )
    one_of(
        pick2,
        lambda i: (i >> 2) * 16 + (i & 3), lambda i: ((i >> 2) ^ 2) * 16 + 4 + (i & 3), lambda i: 64 + (i >> 2) * 16 + (i & 3),
    )
    copies[6].wait()
    pm[pl.ds(32, TILE)] = mid[pl.ds(0, TILE), pl.ds(0, PANEL)]
    ordering(s1, e1, rank1, 4, 1)
    x_landed(0)
    gather_end(0)

    def landing(ref, mine, far, sem, live_rows):
        arrived(codes.at[far], recv_sem.at[sem])
        at = jnp.where(lanes < HALF, codes[mine, 0:1, :], codes[far, 0:1, :] - ROWS)
        for r in range(0, ROWS, 160):
            row = iota((160, ROWS), 0) + r
            hit = row.astype(F32) == at
            if live_rows is not None:
                hit = hit & (row < live_rows)
            ref[pl.ds(r, 160)] = hot(hit)

    def update(front, factor, rows):
        product = mmt(factor[rows], piv[...])
        return (front[rows, pl.ds(PANEL, PANEL)].astype(F32) - product).astype(BF16)

    def far_updates(front, factor, store, other, sem, flip):
        later = []
        for k, (r, n) in enumerate(FAR_CHUNKS):
            at = r - FAR_CHUNKS[0][0]
            store[pl.ds(at, n)] = update(front, factor, pl.ds(r, n))
            later.append((store.at[pl.ds(at, n)], other.at[pl.ds(HALF + at, n)], sem + k, subs(flip)))
        return later

    def own_updates(front, factor, other):
        for r, n in OWN_CHUNKS:
            other[pl.ds(r - TILE, n)] = update(front, factor, pl.ds(r, n))

    def first_part(front, place, other, chunks):
        for r, n in chunks:
            rows = pl.ds(r, n)
            acc[rows] = front[rows, pl.ds(0, PANEL)].astype(F32) + mm(place[rows, pl.ds(0, 256)], other[pl.ds(0, 256)])

    def second_part(place, other, sem, chunks):
        arrived(other.at[pl.ds(HALF, 192)], recv_sem.at[sem])
        for r, n in chunks:
            rows = pl.ds(r, n)
            acc[rows] += mm(place[rows, pl.ds(256, 256)], other[pl.ds(256, 256)])

    def last_part(place, other, sem, chunks, inv, factor, live_rows):
        arrived(other.at[pl.ds(512, 128)], recv_sem.at[sem])
        for r, n in chunks:
            rows = pl.ds(r, n)
            whole = acc[rows] + mm(place[rows, pl.ds(512, 128)], other[pl.ds(512, 128)])
            if live_rows is not None:
                whole = jnp.where((iota((n, PANEL), 0) + r) < live_rows, whole, 0.0)
            factor[rows] = factor_of(whole.astype(BF16), inv)

    pm[pl.ds(0, TILE)] = update(fs, fac, pl.ds(0, TILE))
    send(pm.at[pl.ds(0, TILE)], pm.at[pl.ds(16, TILE)], 10, subs(1))
    later = far_updates(fs, fac, y0, x0, 11, 1)
    copies[8].wait()
    arrived(d1.at[pl.ds(pl.multiple_of((1 - bit0) * 256 + (1 - c) * 128, 128), 128)], recv_sem.at[18])
    arrived(pm.at[pl.ds(48, TILE)], recv_sem.at[4])
    arrived(pm.at[pl.ds(16, TILE)], recv_sem.at[10])
    g[0, pl.ds(0, TILE)] = factor_of(mm(pick1[...], pm[...]).astype(BF16), d1)
    gather_start(1, g.at[0, pl.ds(0, TILE)])
    for part in later:
        send(*part)
    own_updates(fs, fac, x0)
    quarters = (0, 1 - bit0 + 2 * bit1, bit0 + 2 - 2 * bit1, 3 - bit0 - 2 * bit1)
    for f in (1, 2, 3):
        got = d2.at[pl.ds(pl.multiple_of(quarters[f] * 128 + c * 64, 64), 64)]
        arrived(got, recv_sem.at[f])
        send(got, got, 18 + f, inner(0, 0, 1))
    landing(f0, 0, 1, 8, None)
    for r, n in CHUNKS:
        t1[pl.ds(r, n)] = mm(s1[pl.ds(r, n)], f0[...]).astype(BF16)
    ordered(ms, s1, mid, CHUNKS)
    first_part(ms, t1, x0, CHUNKS)
    y_landed(1)
    copies[7].wait()
    pt[pl.ds(64, TILE)] = top[pl.ds(0, TILE), pl.ds(0, PANEL)]
    second_part(t1, x0, 11, CHUNKS)
    x_landed(1)
    last_part(t1, x0, 12, CHUNKS, d1, fac1, None)
    gather_end(1)

    pt[pl.ds(0, TILE)] = update(ms, fac1, pl.ds(0, TILE))
    for f in (2, 1, 3):
        send(pt.at[pl.ds(0, TILE)], pt.at[pl.ds(16 * f, TILE)], 12 + f, subs(f))
    later = far_updates(ms, fac1, y1, x1, 16, 2)
    copies[9].wait()
    for f in (1, 2, 3):
        arrived(d2.at[pl.ds(pl.multiple_of(quarters[f] * 128 + (1 - c) * 64, 64), 64)], recv_sem.at[18 + f])
        arrived(pt.at[pl.ds(64 + 16 * f, TILE)], recv_sem.at[4 + f])
        arrived(pt.at[pl.ds(16 * f, TILE)], recv_sem.at[12 + f])
    g[1, pl.ds(0, TILE)] = factor_of(mm(pick2[...], pt[...]).astype(BF16), d2)
    gather_start(2, g.at[1, pl.ds(0, TILE)])
    for part in later:
        send(*part)
    even = ((0, 320), (320, 320))
    own_updates(ms, fac1, x1)
    landing(f1, 2, 3, 9, live_f[:, 2:3])
    first_part(top, f1, x1, even)
    y_landed(2)
    x_landed(2)
    second_part(f1, x1, 16, even)
    gather_end(2)
    last_part(f1, x1, 17, even, d2, fac2, live_f[:, 2:3])

    results = []
    for r, n in even:
        rows = pl.ds(r, n)
        alive = (iota((n, PANEL), 0) + r) < live_f[:, 2:3]
        product = mmt(fac2[rows], piv[...])
        res[rows] = jnp.where(alive, top[rows, pl.ds(PANEL, PANEL)].astype(F32) - product, 0.0).astype(BF16)
        results.append(pltpu.make_async_copy(res.at[rows], out.at[rows], local_sem.at[len(results)]))
        results[-1].start()
    for copy in sends:
        copy.wait_send()
    for lvl in range(3):
        ref = fs.at[pl.ds(0, 496), pl.ds(0, PANEL)]
        pltpu.make_async_remote_copy(
            src_ref=ref, dst_ref=ref, send_sem=g_send.at[lvl], recv_sem=g_recv.at[lvl, 0],
            device_id=subs(1), device_id_type=MESH,
        ).wait_send()
    for copy in results:
        copy.wait()


def per_device(leaf, mid, top, dinv0, dinv1, dinv2, live_rows, map0, map1):
    hbm = pl.BlockSpec(memory_space=pl.ANY)
    held = lambda *shape: pltpu.VMEM(shape, BF16)
    more = ROWS + TILE
    return pl.pallas_call(
        body,
        name="panel_steps",
        out_shape=jax.ShapeDtypeStruct((ROWS, PANEL), BF16),
        in_specs=[hbm] * 9,
        out_specs=hbm,
        scratch_shapes=[
            held(2, 8, 2, TILE, PANEL),
            held(ROWS, 1024),
            held(ROWS, 1024),
            held(ROWS, 1024),
            held(PANEL, BLOCK),
            pltpu.VMEM((1, 3), jnp.int32),
            pltpu.VMEM((ROWS,), jnp.int32),
            pltpu.VMEM((ROWS,), jnp.int32),
            held(PANEL, BLOCK),
            held(PANEL, BLOCK),
            held(more, ROWS),
            held(more, ROWS),
            held(ROWS, ROWS),
            held(ROWS, ROWS),
            held(more, ROWS),
            held(more, 1024),
            held(more, 1024),
            held(more, PANEL),
            held(more, PANEL),
            held(ROWS, PANEL),
            held(2, PANEL, PANEL),
            held(PANEL, PANEL),
            held(2, PANEL, PANEL),
            held(ROWS, PANEL),
            held(ROWS, PANEL),
            held(HALF, PANEL),
            held(HALF, PANEL),
            held(64, PANEL),
            held(128, PANEL),
            held(TILE, 64),
            held(TILE, 128),
            pltpu.VMEM((more, PANEL), F32),
            held(ROWS, PANEL),
            pltpu.VMEM((4, 8, ROWS), F32),
            pltpu.SemaphoreType.DMA((10,)),
            pltpu.SemaphoreType.DMA((24,)),
            pltpu.SemaphoreType.DMA((22,)),
            pltpu.SemaphoreType.DMA((3,)),
            pltpu.SemaphoreType.DMA((3, 6)),
        ],
        compiler_params=pltpu.CompilerParams(
            collective_id=0, has_side_effects=True, vmem_limit_bytes=60 * 2**20
        ),
    )(leaf, mid, top, dinv0, dinv1, dinv2, live_rows.reshape(1, 3), map0, map1)


def solution(mesh):
    rows = P(("sub", "inner"), None)
    placed = (
        rows, rows, rows, P("sub", None), P("sub", None), P("sub", None),
        P(None, ("sub", "inner")), P(("sub", "inner")), P(("sub", "inner")),
    )
    return jax.shard_map(per_device, mesh=mesh, in_specs=placed, out_specs=rows, check_vma=False)
```

time: 69.1 us -> 57.8 us (0.84)
  local copies, waits for them, and re-layouts: 9.51 us -> 1.97 us
  Pallas kernels: 59.2 us -> 55.7 us
    unnamed x15 -> x1, local copies, waits for them, and re-layouts: 8.13 us -> 1.97 us
    pallas_call x1, Pallas kernels: 59.2 us -> 55.7 us  [per_device(): pl.pallas_call(body, name='panel_steps', out_shape=jax.ShapeDtypeStruct((...]
    reshape x2 -> x0, local copies, waits for them, and re-layouts: 1.38 us -> none  [the longest x1 0.69 us: per_device(): map0.reshape(1, ROWS)]
where the time goes in v2:
time: 57.8 us; the launch traced here: 57.6 us
  Pallas kernels  55.7 us (96%)
  local copies, waits for them, and re-layouts  1.97 us (3%)
    pallas_call x1, Pallas kernels, per_device(): pl.pallas_call(body, name='panel_steps', out_shape=jax.ShapeDtypeStruct((...  55.7 us
    unnamed x1, local copies, waits for them, and re-layouts  1.97 us

profile of v2, /device:TPU:1, one launch (start us, length us, event | category | flops | bytes accessed | tf_op | source)
XLA Modules:
  0.0 57.6 jit_solution(8584775644175596910)
XLA Ops:
  0.0 55.7 %panel_steps.1 = bf16[640,512]{1,0:T(8,128)(2,1)} custom-call(bf16[640,1024]{1,0:T(8,128)(2,1)} %leaf_hbm.1, bf16[640,1024]{1,0:T(8,128)(2,1)} %mid_hbm.1, bf16[640,1024]{1,0:T(8,128)(2,1)} %top_hbm.1, bf16[512,256]{1,0:T(8,128)(2,1)} %dinv0_hbm.1, bf16[256,256]{1,0:T(8,128)(2,1)} %dinv1_hbm.1, bf16[128,256]{1,0:T(8,128)(2,1)} %dinv2_hbm.1, s32[1,3]{1,0:T(1,128)} %bitcast.1, ...), custom_call_target="tpu_custom_call" | custom-call | tf_op jit(solution)/shard_map/panel_steps/pallas_call | solution.py:395
  55.7 2.0 %copy.11 = bf16[640,512]{1,0:T(8,128)(2,1)} copy(bf16[640,512]{1,0:T(8,128)(2,1)} %panel_steps.1) | data formatting | bytes 1310720

commit v3 on v2

--- a/solution.py
+++ b/solution.py
@@ -129,22 +129,23 @@
             return lead.at[1 - xh if flip_x else xh, :, 1 - c if flip_c else c]
         return g.at[lvl - 1, pl.ds(256 * flip_c + 128 * flip_x, 128)]
 
-    def seven(lvl):
-        return lead.at[0, pl.ds(0, 7), 0] if lvl == 0 else g.at[lvl - 1, pl.ds(0, 112)]
+    def four(lvl):
+        return lead.at[0, pl.ds(0, 4), 0] if lvl == 0 else g.at[lvl - 1, pl.ds(16, 64)]
 
     def gather_start(lvl, own):
         for d in FAR_FIRST:
-            g_copy(lvl, own, place(lvl, 0, d, True), 0, inner(0, d, 0))
+            g_copy(lvl, own, place(lvl, 0, d, True), 6 if abs(d) > 2 else 0, inner(0, d, 0))
         for d in FAR_FIRST[3:] + (0,):
             g_copy(lvl, own, place(lvl, 1, d, True), 1, inner(1, d, 0))
 
     def y_landed(lvl):
-        arrived(seven(lvl), g_recv.at[lvl, 0])
+        arrived(three(lvl, 0), g_recv.at[lvl, 6])
         for d in FAR_FIRST[:3]:
             part = place(lvl, 0, d, False)
             for flip_c in (0, 1):
                 to = part if lvl == 0 else g.at[lvl - 1, pl.ds(256 * flip_c + 128 + SLOT[d] * TILE, TILE)]
                 g_copy(lvl, part, to, 4 + flip_c, inner(1, 0, flip_c))
+        arrived(four(lvl), g_recv.at[lvl, 0])
         part = column(lvl, 0, 0)
         g_copy(lvl, part, part if lvl == 0 else column(lvl, 0, 1), 2, inner(0, 0, 1))
 
@@ -354,10 +355,10 @@
         arrived(d2.at[pl.ds(pl.multiple_of(quarters[f] * 128 + (1 - c) * 64, 64), 64)], recv_sem.at[18 + f])
         arrived(pt.at[pl.ds(64 + 16 * f, TILE)], recv_sem.at[4 + f])
         arrived(pt.at[pl.ds(16 * f, TILE)], recv_sem.at[12 + f])
+    for part in later:
+        send(*part)
     g[1, pl.ds(0, TILE)] = factor_of(mm(pick2[...], pt[...]).astype(BF16), d2)
     gather_start(2, g.at[1, pl.ds(0, TILE)])
-    for part in later:
-        send(*part)
     even = ((0, 320), (320, 320))
     own_updates(ms, fac1, x1)
     landing(f1, 2, 3, 9, live_f[:, 2:3])
@@ -437,7 +438,7 @@
             pltpu.SemaphoreType.DMA((24,)),
             pltpu.SemaphoreType.DMA((22,)),
             pltpu.SemaphoreType.DMA((3,)),
-            pltpu.SemaphoreType.DMA((3, 6)),
+            pltpu.SemaphoreType.DMA((3, 7)),
         ],
         compiler_params=pltpu.CompilerParams(
             collective_id=0, has_side_effects=True, vmem_limit_bytes=60 * 2**20

time: 57.8 us -> 57.2 us (0.990)
  Pallas kernels: 55.7 us -> 55 us
    pallas_call x1, Pallas kernels: 55.7 us -> 55 us  [per_device(): pl.pallas_call(body, name='panel_steps', out_shape=jax.ShapeDtypeStruct((...]
where the time goes in v3:
time: 57.2 us; the launch traced here: 57 us
  Pallas kernels  55 us (96%)
  local copies, waits for them, and re-layouts  1.97 us (3%)
    pallas_call x1, Pallas kernels, per_device(): pl.pallas_call(body, name='panel_steps', out_shape=jax.ShapeDtypeStruct((...  55 us
    unnamed x1, local copies, waits for them, and re-layouts  1.97 us

profile of v3, /device:TPU:1, one launch (start us, length us, event | category | flops | bytes accessed | tf_op | source)
XLA Modules:
  0.0 57.0 jit_solution(3028518615584196248)
XLA Ops:
  0.0 55.0 %panel_steps.1 = bf16[640,512]{1,0:T(8,128)(2,1)} custom-call(bf16[640,1024]{1,0:T(8,128)(2,1)} %leaf_hbm.1, bf16[640,1024]{1,0:T(8,128)(2,1)} %mid_hbm.1, bf16[640,1024]{1,0:T(8,128)(2,1)} %top_hbm.1, bf16[512,256]{1,0:T(8,128)(2,1)} %dinv0_hbm.1, bf16[256,256]{1,0:T(8,128)(2,1)} %dinv1_hbm.1, bf16[128,256]{1,0:T(8,128)(2,1)} %dinv2_hbm.1, s32[1,3]{1,0:T(1,128)} %bitcast.1, ...), custom_call_target="tpu_custom_call" | custom-call | tf_op jit(solution)/shard_map/panel_steps/pallas_call | solution.py:396
  55.1 2.0 %copy.11 = bf16[640,512]{1,0:T(8,128)(2,1)} copy(bf16[640,512]{1,0:T(8,128)(2,1)} %panel_steps.1) | data formatting | bytes 1310720

commit v4 on v3

--- a/solution.py
+++ b/solution.py
@@ -307,7 +307,7 @@
             rows = pl.ds(r, n)
             acc[rows] += mm(place[rows, pl.ds(256, 256)], other[pl.ds(256, 256)])
 
-    def last_part(place, other, sem, chunks, inv, factor, live_rows):
+    def last_part(place, other, sem, chunks, inv, factor, live_rows, then=None):
         arrived(other.at[pl.ds(512, 128)], recv_sem.at[sem])
         for r, n in chunks:
             rows = pl.ds(r, n)
@@ -315,6 +315,8 @@
             if live_rows is not None:
                 whole = jnp.where((iota((n, PANEL), 0) + r) < live_rows, whole, 0.0)
             factor[rows] = factor_of(whole.astype(BF16), inv)
+            if then is not None:
+                then(r, n)
 
     pm[pl.ds(0, TILE)] = update(fs, fac, pl.ds(0, TILE))
     send(pm.at[pl.ds(0, TILE)], pm.at[pl.ds(16, TILE)], 10, subs(1))
@@ -347,7 +349,7 @@
     gather_end(1)
 
     pt[pl.ds(0, TILE)] = update(ms, fac1, pl.ds(0, TILE))
-    for f in (2, 1, 3):
+    for f in (3, 2, 1):
         send(pt.at[pl.ds(0, TILE)], pt.at[pl.ds(16 * f, TILE)], 12 + f, subs(f))
     later = far_updates(ms, fac1, y1, x1, 16, 2)
     copies[9].wait()
@@ -367,16 +369,18 @@
     x_landed(2)
     second_part(f1, x1, 16, even)
     gather_end(2)
-    last_part(f1, x1, 17, even, d2, fac2, live_f[:, 2:3])
-
     results = []
-    for r, n in even:
+
+    def finish(r, n):
         rows = pl.ds(r, n)
         alive = (iota((n, PANEL), 0) + r) < live_f[:, 2:3]
         product = mmt(fac2[rows], piv[...])
         res[rows] = jnp.where(alive, top[rows, pl.ds(PANEL, PANEL)].astype(F32) - product, 0.0).astype(BF16)
         results.append(pltpu.make_async_copy(res.at[rows], out.at[rows], local_sem.at[len(results)]))
         results[-1].start()
+
+    last_part(f1, x1, 17, even, d2, fac2, live_f[:, 2:3], finish)
+
     for copy in sends:
         copy.wait_send()
     for lvl in range(3):

time: 57.2 us -> 57.4 us (level)
  no operation moved by 1% of the time
where the time goes in v4:
time: 57.4 us; the launch traced here: 57.3 us
  Pallas kernels  55.3 us (96%)
  local copies, waits for them, and re-layouts  1.97 us (3%)
    pallas_call x1, Pallas kernels, per_device(): pl.pallas_call(body, name='panel_steps', out_shape=jax.ShapeDtypeStruct((...  55.3 us
    unnamed x1, local copies, waits for them, and re-layouts  1.97 us

profile of v4, /device:TPU:1, one launch (start us, length us, event | category | flops | bytes accessed | tf_op | source)
XLA Modules:
  0.0 57.3 jit_solution(5923420352580074956)
XLA Ops:
  0.0 55.3 %panel_steps.1 = bf16[640,512]{1,0:T(8,128)(2,1)} custom-call(bf16[640,1024]{1,0:T(8,128)(2,1)} %leaf_hbm.1, bf16[640,1024]{1,0:T(8,128)(2,1)} %mid_hbm.1, bf16[640,1024]{1,0:T(8,128)(2,1)} %top_hbm.1, bf16[512,256]{1,0:T(8,128)(2,1)} %dinv0_hbm.1, bf16[256,256]{1,0:T(8,128)(2,1)} %dinv1_hbm.1, bf16[128,256]{1,0:T(8,128)(2,1)} %dinv2_hbm.1, s32[1,3]{1,0:T(1,128)} %bitcast.1, ...), custom_call_target="tpu_custom_call" | custom-call | tf_op jit(solution)/shard_map/panel_steps/pallas_call | solution.py:400
  55.3 2.0 %copy.11 = bf16[640,512]{1,0:T(8,128)(2,1)} copy(bf16[640,512]{1,0:T(8,128)(2,1)} %panel_steps.1) | data formatting | bytes 1310720
